TPU v7x, 1024 devices: a whole 8x8x8 slice. The times are simulated.
1024 devices in a mesh: dp: 64 (over y, x), tensor: 16 (over z, core).
Axes of the slice: x: 8, y: 8, z: 8, core: 2. Of those that a mesh axis runs over, the one named last changes fastest.
Arguments:
- activations: bfloat16 [8192, 4096], P('dp'), may hold values from -6 to 6
- out_grads: bfloat16 [8192, 28672], P('dp', 'tensor'), may hold values from -1536 to 1536
- token_ids: int32 [8192], P('dp'), may hold values from 0 to 128255, as said below
- prev_acts: bfloat16 [8192, 4096], P('dp'), may hold values from -6 to 6
- prev_grads: bfloat16 [8192, 28672], P('dp', 'tensor'), may hold values from -1536 to 1536
- prev_basis: float32 [4096, 32], replicated, may hold values from -0.09375 to 0.09375
- warm_start: float32 [28672, 32], P('tensor'), may hold values from -18 to 18
Outputs:
- update_rows: bfloat16 [4096, 28672], P('dp', 'tensor')
- next_start: float32 [28672, 32], P('tensor')
Inputs may be any that keep to these rules, and one draw needn't show every extreme that they name: `token_ids`: each replica's block of 128 ids ends in 0 to 64 padding ids 0; the other ids are 1 or more.
All inputs are finite; a program needn't handle non-finite values.
Results may differ from a plain program's by a relative error of at most 0.0017.
Values sent between devices are 32-bit elements; how exact they have to be, the bound alone decides.
A program may use at most 32 MiB of HBM per device.

v0:
```python
import jax
import jax.numpy as jnp
from jax import lax
from jax.sharding import PartitionSpec as P


def fdot(first, second):
    return jnp.dot(
        first, second, precision=lax.Precision.HIGHEST, preferred_element_type=jnp.float32
    )


def orthonormal(left):
    square = fdot(left.T, left)
    factor = jnp.linalg.cholesky(square)
    return jax.scipy.linalg.solve_triangular(factor, left.T, lower=True).T


def shards(activations, out_grads, token_ids, prev_acts, prev_grads, prev_basis, warm_start):
    replicas = lax.axis_size("dp")
    tok_count = activations.shape[0]
    inv_tokens = 1.0 / (replicas * tok_count)
    token_mask = (token_ids != 0).astype(jnp.float32)[:, None]
    live_local = jnp.sum(token_mask)
    proj_now = fdot(out_grads, warm_start)
    proj_old = fdot(prev_grads, warm_start)
    warm_gram = fdot(warm_start.T, warm_start)
    row_count = prev_basis.shape[0] // replicas
    row_start = lax.axis_index("dp") * row_count
    part_now = fdot(activations.T, proj_now * token_mask)
    part_old = fdot(prev_acts.T, proj_old) * inv_tokens - fdot(prev_basis, warm_gram) / replicas
    live_share = jnp.where(lax.axis_index("tensor") == 0, live_local, 0.0)
    part_now, part_old, live_total = lax.psum((part_now, part_old, live_share), ("dp", "tensor"))
    left = part_now / live_total + part_old
    basis = orthonormal(left)
    back_now = fdot(activations, basis) * token_mask
    back_old = fdot(prev_acts, basis)
    cross = fdot(prev_basis.T, basis)
    my_basis = lax.dynamic_slice_in_dim(basis, row_start, row_count, 0)
    right_part = (
        fdot(out_grads.T, back_now) / live_total
        + fdot(prev_grads.T, back_old) * inv_tokens
        - fdot(warm_start, cross) / replicas
    )
    next_start = lax.psum(right_part, "dp")
    update_rows = fdot(my_basis, next_start.T).astype(jnp.bfloat16)
    return (update_rows, next_start)


def solution(mesh):
    in_specs = (
        P("dp", None),
        P("dp", "tensor"),
        P("dp"),
        P("dp", None),
        P("dp", "tensor"),
        P(),
        P("tensor", None),
    )
    out_specs = (P("dp", "tensor"), P("tensor", None))
    return jax.shard_map(shards, mesh=mesh, in_specs=in_specs, out_specs=out_specs, check_vma=False)
```

profile of v0, /device:TPU:1, one launch (start us, length us, event | category | flops | bytes accessed | tf_op | source)
XLA Modules:
  0.0 500.6 jit_solution(2680817620666698708)
XLA Ops:
  7.2 0.0 all-reduce.6.cloned.1.call-start
  7.2 0.7 compare_convert_fusion
  8.0 1.4 fusion.14
  9.4 1.6 fusion.13
  11.0 0.5 convolution_multiply_fusion.4
  11.5 1.4 convolution_bitcast_fusion
  13.0 0.6 convolution_multiply_fusion.1
  13.6 0.4 copy-done.3
  14.0 1.5 fusion.1
  15.5 0.0 all-reduce.6.cloned.1.call-update
  15.5 0.0 all-reduce.4.cloned.1.call-start
  15.5 0.6 copy-done.8
  16.2 0.6 fusion.11
  17.4 129.5 %psum.29 = f32[]{:T(128)} all-reduce(f32[]{:T(128)S(6)} %select_n.11), channel_id=1, replica_groups=mesh['dp'=64,'tensor'=16] {'dp','tensor'}, use_global_device_ids=true, to_apply=%region_2.3 | all-reduce | flops 1 | bytes 8 | tf_op jit(solution)/shard_map/psum | solution.py:33
  146.9 172.7 %all-reduce.6.cloned.1.call-done = (f32[4096,32]{0,1:T(8,128)}, f32[4096,32]{0,1:T(8,128)}) async-done(((f32[4096,32]{0,1:T(8,128)}, f32[4096,32]{0,1:T(8,128)}), (f32[4096,32]{0,1:T(8,128)}, f32[4096,32]{0,1:T(8,128)})) %all-reduce.6.cloned.1.call-update) | async-done | bytes 1048592 | tf_op jit(solution)/shard_map/psum | solution.py:33
  319.7 2.8 fusion.12
  322.5 0.1 copy.9
  322.5 2.9 cholesky.16
  325.5 0.6 compare_reduce_fusion
  326.1 0.7 fusion.5
  326.8 2.4 custom-call.7
  329.2 2.5 fusion.6
  331.7 1.1 convolution_multiply_fusion.5
  332.8 0.6 fusion.16
  333.4 1.1 fusion.15
  334.5 0.9 convolution_divide_fusion
  335.4 0.3 convolution_multiply_fusion.3
  335.8 0.7 copy-done.4
  336.4 1.0 fusion.4
  337.5 153.3 %all-reduce.4.cloned.1.call-done = f32[1792,32]{0,1:T(8,128)} async-done(((f32[1792,32]{0,1:T(8,128)}), f32[1792,32]{0,1:T(8,128)}) %all-reduce.4.cloned.1.call-update) | async-done | bytes 229392 | tf_op jit(solution)/shard_map/psum | solution.py:45
  490.7 2.3 convolution_convert_fusion
  493.1 0.7 copy.13
  (18 shorter events, 0.1 us)
Async XLA Ops:
  7.2 4.4 copy-start
  7.2 312.5 %all-reduce.6.cloned.1.call-start = ((), (), s32[]{:S(2)}) async-start(), calls=%async_computation.1 | async-start | bytes 2097152 | tf_op jit(solution)/shard_map/psum | solution.py:33
  8.0 1.4 copy-start.1
  9.4 1.6 copy-start.6
  11.0 1.9 copy-start.2
  13.0 1.0 copy-start.3
  15.5 475.3 %all-reduce.4.cloned.1.call-start = ((), (), s32[]{:S(2)}) async-start(), calls=%async_computation | async-start | bytes 458752 | tf_op jit(solution)/shard_map/psum | solution.py:45
  15.5 0.7 copy-start.8
  333.4 1.1 copy-start.7
  335.4 1.0 copy-start.4
  490.7 2.3 copy-start.5
Sparse Core Ops, SparseCore 0:
  15.6 304.0 all-reduce.5
  337.6 153.0 all-reduce.3
where the time goes:
time: 504 us; the launch traced here: 501 us
  waiting for transfers between devices  326 us (65%)
  blocking collectives  129 us (26%)
  matrix products  19.6 us (4%)
  between operations  14.9 us (3%)
  other arithmetic  8.03 us (2%)
    psum x1, waiting for transfers between devices, shards(): lax.psum((part_now, part_old, live_share), ('dp', 'tensor'))  173 us
    psum x1, waiting for transfers between devices, shards(): next_start = lax.psum(right_part, 'dp')  153 us
    psum x1, blocking collectives, shards(): lax.psum((part_now, part_old, live_share), ('dp', 'tensor'))  129 us
    dot_general x14, matrix products, fdot(): jnp.dot(first, second, precision=lax.Precision.HIGHEST, preferred_element...  17.1 us
  transfers between devices with their start and end apart: 2, of which 2 were waited for; matrix products, arithmetic and copies ran while one was open for 0% of the time, Pallas kernels for 0%

commit v1 on v0

v1 whole, which is shorter than its diff:
```python
import jax
import jax.numpy as jnp
from jax import lax
from jax.experimental import pallas as pl
from jax.experimental.pallas import tpu as pltpu
from jax.sharding import PartitionSpec as P

MESH = pl.DeviceIdType.MESH
F32, BF16 = jnp.float32, jnp.bfloat16
HIGHEST = lax.Precision.HIGHEST

SIDE = 8
NT = 16
REPLICAS = 64
TOK = 128
RANK = 32
OWN = RANK // NT
DIM = 4096
FF = 1792
DCH = DIM // SIDE
FAR = (4, 3, 5, 2, 6, 1, 7)
INV_TOKENS = 1.0 / (REPLICAS * TOK)
ACOLS = 1024
BCOLS = 384


def nt_dot(first, second):
    return lax.dot_general(first, second, (((1,), (1,)), ((), ())), preferred_element_type=F32)


def dot32(first, second, dims=((1,), (0,))):
    return lax.dot_general(first, second, (dims, ((), ())), precision=HIGHEST, preferred_element_type=F32)


def pieces(value):
    high = value.astype(BF16).astype(F32)
    rest = value - high
    mid = rest.astype(BF16).astype(F32)
    low = (rest - mid).astype(BF16).astype(F32)
    return high, mid, low


def total(ref, count):
    acc = ref[0]
    for k in range(1, count):
        acc = acc + ref[k]
    return acc


def inverse_factor(gram):
    rows = lax.broadcasted_iota(jnp.int32, (RANK, 128), 0)
    lanes = lax.broadcasted_iota(jnp.int32, (RANK, 128), 1)
    eye = (lanes == rows + RANK).astype(F32)
    work = jnp.concatenate([gram, jnp.zeros((RANK, 128 - RANK), F32)], axis=1) + eye
    for k in range(RANK):
        row = work[k : k + 1, :]
        pivot = row[:, k : k + 1]
        column = work[:, k : k + 1]
        scaled = row * (1.0 / pivot)
        root = row * lax.rsqrt(pivot)
        below = work - column * scaled
        work = jnp.where(rows > k, below, jnp.where(rows == k, root, work))
    return work[:, RANK : 2 * RANK]


def kernel(
    x_hbm, y_hbm, ids_ref, u_hbm, v_hbm, bt_hbm, wt_hbm,
    upd_ref, nxt_ref,
    xub, yvw, bt, wt,
    a_send, a_recv, l_send, l_recv, b_send, b_recv, c_send, c_recv, d_send, d_recv,
    gb, lf, g_send, g_recv, back, mine, crs, cw,
    ea_send, ea_recv, eb_send, eb_recv, fa_send, fa_recv, fb_send, fb_recv,
    ga_send, ga_recv, gb_send, gb_recv,
    load_sem, send_sem, recv_sem,
):
    dp, t = lax.axis_index("dp"), lax.axis_index("tensor")
    y, x = dp // SIDE, lax.rem(dp, SIDE)
    z, core = t // 2, lax.rem(t, 2)

    loads = []
    for k, (src, dst) in enumerate(
        (
            (wt_hbm, wt),
            (y_hbm, yvw.at[pl.ds(0, TOK)]),
            (v_hbm, yvw.at[pl.ds(TOK, TOK)]),
            (bt_hbm, bt),
            (x_hbm, xub.at[pl.ds(0, TOK)]),
            (u_hbm, xub.at[pl.ds(TOK, TOK)]),
        )
    ):
        copy = pltpu.make_async_copy(src, dst, load_sem.at[k])
        copy.start()
        loads.append(copy)

    ring = [lax.rem(jnp.int32(k) + x, SIDE) for k in FAR]
    xs = [(k, (y * SIDE + k, t)) for k in ring]
    ring = [lax.rem(jnp.int32(k) + y, SIDE) for k in FAR]
    ys = [(k, (k * SIDE + x, t)) for k in ring]
    ts = []
    for k in FAR:
        zk = lax.rem(z + k, SIDE)
        ts += [(zk * 2, (dp, zk * 2)), (zk * 2 + 1, (dp, zk * 2 + 1))]
    ts.append((t + 1 - 2 * core, (dp, t + 1 - 2 * core)))

    barrier = pltpu.get_barrier_semaphore()
    for _, peer in ts + ys + xs:
        pl.semaphore_signal(barrier, inc=1, device_id=peer, device_id_type=MESH)

    def send(phase, src, dst, peer):
        pltpu.make_async_remote_copy(
            src_ref=src, dst_ref=dst, send_sem=send_sem.at[phase], recv_sem=recv_sem.at[phase], device_id=peer, device_id_type=MESH
        ).start()

    def arrived(phase, ref, count):
        whole = ref.at[pl.ds(0, count)]
        pltpu.make_async_copy(whole, whole, recv_sem.at[phase]).wait()

    def left(phase, ref, count):
        whole = ref.at[pl.ds(0, count)]
        pltpu.make_async_copy(whole, whole, send_sem.at[phase]).wait()

    mask = (ids_ref[...] != 0).astype(F32)
    l_send[...] = jnp.broadcast_to(jnp.sum(mask, axis=1, keepdims=True), (1, 128))
    loads[0].wait()
    for k, piece in enumerate(pieces(wt[...])):
        yvw[2 * TOK + k * RANK : 2 * TOK + (k + 1) * RANK, :] = piece.astype(BF16)
    yvw[2 * TOK + 3 * RANK :, :] = jnp.zeros((RANK, FF), BF16)
    loads[1].wait()
    loads[2].wait()
    proj = nt_dot(yvw[2 * TOK : 2 * TOK + 3 * RANK, :], yvw[...])
    proj = proj[:RANK] + proj[RANK : 2 * RANK] + proj[2 * RANK :]
    for k in range(NT):
        own = proj[OWN * k : OWN * (k + 1)]
        a_send[k] = jnp.concatenate([own[:, :128], own[:, 128:256], own[:, 256:], own[:, 256:]], axis=0)
    pl.semaphore_wait(barrier, len(ts + ys + xs))

    for k, peer in ts:
        send(0, a_send.at[k], a_recv.at[t], peer)
    for _, peer in xs:
        send(1, l_send, l_recv.at[x], peer)
    a_recv[t] = a_send[t]
    l_recv[x] = l_send[...]
    loads[3].wait()
    for k, piece in enumerate(pieces(bt[...])):
        xub[2 * TOK + k * RANK : 2 * TOK + (k + 1) * RANK, :] = piece.astype(BF16)
    xub[2 * TOK + 3 * RANK :, :] = jnp.zeros((RANK, DIM), BF16)
    loads[4].wait()
    loads[5].wait()
    arrived(0, a_recv, NT - 1)
    own = total(a_recv, NT)
    rows = lax.broadcasted_iota(jnp.int32, (2 * OWN, TOK), 0)
    now = jnp.where(rows < OWN, own[: 2 * OWN] * mask, 0.0)
    old = jnp.where(rows >= OWN, own[: 2 * OWN] * INV_TOKENS, 0.0)
    stacked = jnp.concatenate([now, old], axis=1)
    stacked = jnp.concatenate([*pieces(stacked), jnp.zeros((2 * OWN, 2 * TOK), F32)], axis=0).astype(BF16)
    arrived(1, l_recv, SIDE - 1)
    live_x = jnp.broadcast_to(total(l_recv, SIDE), (2 * OWN, 128))

    def left_chunk(k):
        part = jnp.dot(stacked, xub[: 2 * TOK, pl.ds(pl.multiple_of(k * DCH, DCH), DCH)], preferred_element_type=F32)
        return part[: 2 * OWN] + part[2 * OWN : 4 * OWN] + part[4 * OWN : 6 * OWN]

    for k, peer in ys:
        b_send[k, :, :DCH] = left_chunk(k)
        b_send[k, :, DCH:] = live_x
        send(2, b_send.at[k], b_recv.at[y], peer)
    b_recv[y, :, :DCH] = left_chunk(y)
    b_recv[y, :, DCH:] = live_x
    square = own[4:6, :RANK] + own[4:6, RANK : 2 * RANK] + own[4:6, 2 * RANK : 3 * RANK]
    gb[...] = dot32(square, bt[...])
    arrived(2, b_recv, SIDE - 1)
    summed = total(b_recv, SIDE)
    inv_live = 1.0 / summed[:1, DCH : DCH + 128]
    inv_wide = jnp.concatenate([inv_live] * (DCH // 128), axis=1)
    chunk = summed[:OWN, :DCH] * inv_wide + summed[OWN:, :DCH]
    c_send[...] = chunk
    for _, peer in xs:
        send(3, c_send, c_recv.at[x], peer)
    c_recv[x] = chunk
    arrived(3, c_recv, SIDE - 1)

    chunk = total(c_recv, SIDE)
    d_send[...] = chunk
    for _, peer in ys:
        send(4, d_send, d_recv.at[y], peer)
    d_recv[y] = chunk
    arrived(4, d_recv, SIDE - 1)
    acc = jnp.zeros((16, 3 * 128), F32)
    for k in range(SIDE):
        part = d_recv[k] - gb[:, k * DCH : (k + 1) * DCH]
        lf[:, k * DCH : (k + 1) * DCH] = part
        part = jnp.concatenate([*pieces(part), jnp.zeros((16 - 3 * OWN, DCH), F32)], axis=0).astype(BF16)
        acc = acc + nt_dot(part, xub[:, k * DCH : (k + 1) * DCH])
    acc = acc[:OWN] + acc[OWN : 2 * OWN] + acc[2 * OWN : 3 * OWN]

    my_lanes = pl.ds(pl.multiple_of(dp // 2 * 128, 128), 128)
    tile = jnp.concatenate(
        [acc[:, :128] * (mask * inv_live), acc[:, 128:256] * INV_TOKENS, lf[:, my_lanes], acc[:, 256:]], axis=0
    )
    g_send[...] = tile
    for _, peer in ts:
        send(5, g_send, g_recv.at[t], peer)
    g_recv[t] = tile
    arrived(5, g_recv, NT - 1)
    for k in range(NT):
        tile = g_recv[k]
        at = slice(OWN * k, OWN * (k + 1))
        back[at, :128] = tile[:2]
        back[at, 128:] = tile[2:4]
        mine[at, :] = tile[4:6]
        crs[at, :] = tile[6:8]

    stacked = jnp.concatenate(pieces(back[...]), axis=0).astype(BF16)

    def right_part(first, width):
        part = jnp.dot(stacked, yvw[: 2 * TOK, pl.ds(first, width)], preferred_element_type=F32)
        return part[:RANK] + part[RANK : 2 * RANK] + part[2 * RANK :]

    for k in range(0, SIDE, 2):
        part = right_part(k * 128, 256)
        ea_send[k] = part[:, :128]
        ea_send[k + 1] = part[:, 128:]
    for k, peer in ys:
        send(6, ea_send.at[k], ea_recv.at[y], peer)
    half = lax.rem(dp, 2)
    lanes = lax.broadcasted_iota(jnp.int32, (RANK, 128), 1)
    my_rows = jnp.where(lanes // 64 == half, mine[...], 0.0)
    gram = dot32(my_rows, my_rows, ((1,), (1,)))
    gram = jnp.concatenate([gram[8 * k : 8 * (k + 1)] for k in range(RANK // 8)], axis=1)
    for h in range(2):
        part = right_part(ACOLS + h * BCOLS, BCOLS)
        for k in range(RANK // 8):
            eb_send[2 * k + h, :, :BCOLS] = part[8 * k : 8 * (k + 1)]
            eb_send[2 * k + h, :, BCOLS:] = gram
    for k, peer in xs:
        send(7, eb_send.at[k], eb_recv.at[x], peer)
    ea_recv[y] = ea_send[y]
    eb_recv[x] = eb_send[x]
    cross = crs[:, :RANK] + crs[:, RANK : 2 * RANK] + crs[:, 2 * RANK : 3 * RANK]
    cw[...] = dot32(cross, wt[...])
    arrived(6, ea_recv, SIDE - 1)
    part = total(ea_recv, SIDE)
    fa_send[...] = part
    for _, peer in xs:
        send(8, fa_send, fa_recv.at[x], peer)
    fa_recv[x] = part
    arrived(7, eb_recv, SIDE - 1)
    part = total(eb_recv, SIDE)
    fb_send[...] = part
    for _, peer in ys:
        send(9, fb_send, fb_recv.at[y], peer)
    fb_recv[y] = part
    arrived(8, fa_recv, SIDE - 1)
    part = total(fa_recv, SIDE)
    ga_send[...] = part
    for _, peer in ys:
        send(10, ga_send, ga_recv.at[y], peer)
    ga_recv[y] = part
    arrived(9, fb_recv, SIDE - 1)
    part = total(fb_recv, SIDE)
    gb_send[...] = part[:, :BCOLS]
    for _, peer in xs:
        send(11, gb_send, gb_recv.at[x], peer)
    gb_recv[x] = part[:, :BCOLS]
    packed = part[:, BCOLS:]
    gram = jnp.concatenate([packed[:, RANK * k : RANK * (k + 1)] for k in range(RANK // 8)], axis=0)
    inverse = inverse_factor(gram)
    basis = dot32(inverse, mine[...])
    rows = dot32(basis, inverse, ((0,), (0,)))
    rows = jnp.where(half == 0, rows[:64], rows[64:])
    both = jnp.concatenate([inverse, rows], axis=0)

    def finish(first, raw):
        width = raw.shape[1]
        out = dot32(both, raw - cw[:, first : first + width])
        nxt_ref[:, first : first + width] = out[:RANK]
        upd_ref[:, first : first + width] = out[RANK:].astype(BF16)

    arrived(10, ga_recv, SIDE - 1)
    for k in range(0, SIDE, 2):
        finish(k * 128, jnp.concatenate([ga_recv[k], ga_recv[k + 1]], axis=1))
    arrived(11, gb_recv, SIDE - 1)
    for h in range(2):
        finish(ACOLS + h * BCOLS, jnp.concatenate([gb_recv[2 * k + h] for k in range(RANK // 8)], axis=0))

    for phase, (ref, count) in enumerate(
        (
            (a_recv, NT - 1), (l_recv, SIDE - 1), (b_recv, SIDE - 1), (c_recv, SIDE - 1), (d_recv, SIDE - 1), (g_recv, NT - 1),
            (ea_recv, SIDE - 1), (eb_recv, SIDE - 1), (fa_recv, SIDE - 1), (fb_recv, SIDE - 1), (ga_recv, SIDE - 1), (gb_recv, SIDE - 1),
        )
    ):
        left(phase, ref, count)


def shards(activations, out_grads, token_ids, prev_acts, prev_grads, prev_basis, warm_start):
    def vmem(*shape, dtype=F32):
        return pltpu.VMEM(shape, dtype)

    hbm = pl.BlockSpec(memory_space=pl.ANY)
    local = pl.BlockSpec(memory_space=pltpu.VMEM)
    update, start = pl.pallas_call(
        kernel,
        out_shape=(jax.ShapeDtypeStruct((DIM // REPLICAS, FF), BF16), jax.ShapeDtypeStruct((RANK, FF), F32)),
        in_specs=[hbm, hbm, local, hbm, hbm, hbm, hbm],
        out_specs=(local, local),
        scratch_shapes=[
            vmem(3 * TOK, DIM, dtype=BF16), vmem(3 * TOK, FF, dtype=BF16), vmem(RANK, DIM), vmem(RANK, FF),
            vmem(NT, 8, 128), vmem(NT, 8, 128), vmem(1, 128), vmem(SIDE, 1, 128),
            vmem(SIDE, 2 * OWN, DCH + 128), vmem(SIDE, 2 * OWN, DCH + 128),
            vmem(OWN, DCH), vmem(SIDE, OWN, DCH), vmem(OWN, DCH), vmem(SIDE, OWN, DCH),
            vmem(OWN, DIM), vmem(OWN, DIM), vmem(8, 128), vmem(NT, 8, 128),
            vmem(RANK, 2 * TOK), vmem(RANK, 128), vmem(RANK, 128), vmem(RANK, FF),
            vmem(SIDE, RANK, 128), vmem(SIDE, RANK, 128), vmem(SIDE, 8, BCOLS + 128), vmem(SIDE, 8, BCOLS + 128),
            vmem(RANK, 128), vmem(SIDE, RANK, 128), vmem(8, BCOLS + 128), vmem(SIDE, 8, BCOLS + 128),
            vmem(RANK, 128), vmem(SIDE, RANK, 128), vmem(8, BCOLS), vmem(SIDE, 8, BCOLS),
            pltpu.SemaphoreType.DMA((6,)), pltpu.SemaphoreType.DMA((12,)), pltpu.SemaphoreType.DMA((12,)),
        ],
        compiler_params=pltpu.CompilerParams(collective_id=0, has_side_effects=True, vmem_limit_bytes=40 * 2**20),
        cost_estimate=pl.CostEstimate(flops=10**9, bytes_accessed=5 * 10**6, transcendentals=0),
    )(
        activations, out_grads, token_ids.reshape(1, TOK), prev_acts, prev_grads, prev_basis.T, warm_start.T
    )
    return update, start.T


def solution(mesh):
    in_specs = (P("dp", None), P("dp", "tensor"), P("dp"), P("dp", None), P("dp", "tensor"), P(), P("tensor", None))
    out_specs = (P("dp", "tensor"), P("tensor", None))
    return jax.shard_map(shards, mesh=mesh, in_specs=in_specs, out_specs=out_specs, check_vma=False)
```

time: 504 us -> 74.4 us (0.15)
  waiting for transfers between devices: 326 us -> 0 us
  blocking collectives: 129 us -> 0 us
  Pallas kernels: 0 us -> 63.8 us
  matrix products: 19.6 us -> 0 us
  between operations: 14.9 us -> 0.66 us
  other arithmetic: 8.03 us -> 0 us
  local copies, waits for them, and re-layouts: 2.58 us -> 8.49 us
    psum x2 -> x0, waiting for transfers between devices: 326 us -> none  [the longest x1 173 us: shards(): lax.psum((part_now, part_old, live_share), ('dp', 'tensor'))]
    psum x1 -> x0, blocking collectives: 129 us -> none  [shards(): lax.psum((part_now, part_old, live_share), ('dp', 'tensor'))]
    pallas_call x0 -> x1, Pallas kernels: none -> 63.8 us  [shards(): pl.pallas_call(kernel, out_shape=(jax.ShapeDtypeStruct((DIM // REPLICAS,...]
    dot_general x14 -> x0, matrix products: 17.1 us -> none  [fdot(): jnp.dot(first, second, precision=lax.Precision.HIGHEST, preferred_element...]
    another operation x5 -> x0, other arithmetic: 6.68 us -> none  [the longest x3 3.6 us: orthonormal(): factor = jnp.linalg.cholesky(square)]
    unnamed x19 -> x16, local copies, waits for them, and re-layouts: 2.51 us -> 8.49 us
  transfers between devices with their start and end apart: 2 -> 0, of which waited for: 2 -> 0; matrix products, arithmetic and copies ran while one was open for 0% -> 0% of each run, Pallas kernels for 0% -> 0%
where the time goes in v1:
time: 74.4 us; the launch traced here: 73 us
  Pallas kernels  63.8 us (86%)
  local copies, waits for them, and re-layouts  8.49 us (11%)
    pallas_call x1, Pallas kernels, shards(): pl.pallas_call(kernel, out_shape=(jax.ShapeDtypeStruct((DIM // REPLICAS,...  63.8 us
    unnamed x16, local copies, waits for them, and re-layouts  8.49 us

profile of v1, /device:TPU:1, one launch (start us, length us, event | category | flops | bytes accessed | tf_op | source)
XLA Modules:
  0.0 73.0 jit_solution(3602192648213808812)
XLA Ops:
  0.6 0.0 copy-start.6
  0.6 0.6 copy-done.6
  1.3 0.0 copy-start
  1.3 1.2 %copy-done = bf16[128,4096]{1,0:T(8,128)(2,1)S(1)} copy-done((bf16[128,4096]{1,0:T(8,128)(2,1)S(1)}, bf16[128,4096]{1,0:T(8,128)(2,1)}, u32[]{:S(2)}) %copy-start) | copy-done | bytes 1048600
  2.5 0.0 copy-start.1
  2.5 1.2 %copy-done.1 = bf16[128,4096]{1,0:T(8,128)(2,1)S(1)} copy-done((bf16[128,4096]{1,0:T(8,128)(2,1)S(1)}, bf16[128,4096]{1,0:T(8,128)(2,1)}, u32[]{:S(2)}) %copy-start.1) | copy-done | bytes 1048600
  3.7 0.0 copy-start.2
  3.7 1.0 %copy-done.2 = f32[4096,32]{0,1:T(8,128)S(1)} copy-done((f32[4096,32]{0,1:T(8,128)S(1)}, f32[4096,32]{0,1:T(8,128)}, u32[]{:S(2)}) %copy-start.2) | copy-done | bytes 524312
  4.8 0.0 copy-start.3
  4.8 1.0 %copy-done.3 = bf16[128,1792]{1,0:T(8,128)(2,1)S(1)} copy-done((bf16[128,1792]{1,0:T(8,128)(2,1)S(1)}, bf16[128,1792]{1,0:T(8,128)(2,1)}, u32[]{:S(2)}) %copy-start.3) | copy-done | bytes 458776
  5.8 0.0 copy-start.4
  5.8 1.0 %copy-done.4 = bf16[128,1792]{1,0:T(8,128)(2,1)S(1)} copy-done((bf16[128,1792]{1,0:T(8,128)(2,1)S(1)}, bf16[128,1792]{1,0:T(8,128)(2,1)}, u32[]{:S(2)}) %copy-start.4) | copy-done | bytes 458776
  6.8 0.0 copy-start.5
  6.8 0.9 %copy-done.5 = f32[1792,32]{0,1:T(8,128)S(1)} copy-done((f32[1792,32]{0,1:T(8,128)S(1)}, f32[1792,32]{0,1:T(8,128)}, u32[]{:S(2)}) %copy-start.5) | copy-done | bytes 229400
  7.8 63.8 %shard_map.86 = (bf16[64,1792]{1,0:T(8,128)(2,1)S(1)}, f32[32,1792]{1,0:T(8,128)S(1)}) custom-call(bf16[128,4096]{1,0:T(8,128)(2,1)S(1)} %copy-done, bf16[128,1792]{1,0:T(8,128)(2,1)S(1)} %copy-done.3, s32[1,128]{1,0:T(1,128)S(1)} %bitcast.7, bf16[128,4096]{1,0:T(8,128)(2,1)S(1)} %copy-done.1, bf16[128,1792]{1,0:T(8,128)(2,1)S(1)} %copy-done.4, ...), custom_call_target="tpu_custom_call" | custom-call | flops 1000000000 | bytes 5000000 | tf_op jit(solution)/shard_map/pallas_call | solution.py:301
  71.6 0.7 copy.11
  72.3 0.7 copy.12
Async XLA Ops:
  0.6 0.7 copy-start.6
  1.3 1.2 %copy-start = (bf16[128,4096]{1,0:T(8,128)(2,1)S(1)}, bf16[128,4096]{1,0:T(8,128)(2,1)}, u32[]{:S(2)}) copy-start(bf16[128,4096]{1,0:T(8,128)(2,1)} %x_hbm.1) | copy-start | bytes 3145732
  2.5 1.2 %copy-start.1 = (bf16[128,4096]{1,0:T(8,128)(2,1)S(1)}, bf16[128,4096]{1,0:T(8,128)(2,1)}, u32[]{:S(2)}) copy-start(bf16[128,4096]{1,0:T(8,128)(2,1)} %u_hbm.1) | copy-start | bytes 3145732
  3.7 1.0 %copy-start.2 = (f32[4096,32]{0,1:T(8,128)S(1)}, f32[4096,32]{0,1:T(8,128)}, u32[]{:S(2)}) copy-start(f32[4096,32]{0,1:T(8,128)} %param.12) | copy-start | bytes 1572868
  4.8 1.0 %copy-start.3 = (bf16[128,1792]{1,0:T(8,128)(2,1)S(1)}, bf16[128,1792]{1,0:T(8,128)(2,1)}, u32[]{:S(2)}) copy-start(bf16[128,1792]{1,0:T(8,128)(2,1)} %y_hbm.1) | copy-start | bytes 1376260
  5.8 1.0 %copy-start.4 = (bf16[128,1792]{1,0:T(8,128)(2,1)S(1)}, bf16[128,1792]{1,0:T(8,128)(2,1)}, u32[]{:S(2)}) copy-start(bf16[128,1792]{1,0:T(8,128)(2,1)} %v_hbm.1) | copy-start | bytes 1376260
  6.8 0.9 %copy-start.5 = (f32[1792,32]{0,1:T(8,128)S(1)}, f32[1792,32]{0,1:T(8,128)}, u32[]{:S(2)}) copy-start(f32[1792,32]{0,1:T(8,128)} %param.13) | copy-start | bytes 688132

commit v2 on v1

--- a/solution.py
+++ b/solution.py
@@ -64,18 +64,33 @@
 
 
 def kernel(
-    x_hbm, y_hbm, ids_ref, u_hbm, v_hbm, bt_hbm, wt_hbm,
+    x_hbm, y_hbm, ids_hbm, u_hbm, v_hbm, bt_hbm, wt_hbm,
     upd_ref, nxt_ref,
     xub, yvw, bt, wt,
     a_send, a_recv, l_send, l_recv, b_send, b_recv, c_send, c_recv, d_send, d_recv,
     gb, lf, g_send, g_recv, back, mine, crs, cw,
     ea_send, ea_recv, eb_send, eb_recv, fa_send, fa_recv, fb_send, fb_recv,
     ga_send, ga_recv, gb_send, gb_recv,
-    load_sem, send_sem, recv_sem,
+    h_send, h_recv, p_send, p_recv, q_send, q_recv, lp,
+    ids, load_sem, send_sem, recv_sem, slot_sem,
 ):
     dp, t = lax.axis_index("dp"), lax.axis_index("tensor")
     y, x = dp // SIDE, lax.rem(dp, SIDE)
     z, core = t // 2, lax.rem(t, 2)
+
+    ring = [lax.rem(jnp.int32(k) + x, SIDE) for k in FAR]
+    xs = [(k, (y * SIDE + k, t)) for k in ring]
+    ring = [lax.rem(jnp.int32(k) + y, SIDE) for k in FAR]
+    ys = [(k, (k * SIDE + x, t)) for k in ring]
+    ts = []
+    for k in FAR:
+        zk = lax.rem(z + k, SIDE)
+        ts += [(zk * 2, (dp, zk * 2)), (zk * 2 + 1, (dp, zk * 2 + 1))]
+    ts.append((t + 1 - 2 * core, (dp, t + 1 - 2 * core)))
+
+    barrier = pltpu.get_barrier_semaphore()
+    for _, peer in ts + ys + xs:
+        pl.semaphore_signal(barrier, inc=1, device_id=peer, device_id_type=MESH)
 
     loads = []
     for k, (src, dst) in enumerate(
@@ -86,29 +101,17 @@
             (bt_hbm, bt),
             (x_hbm, xub.at[pl.ds(0, TOK)]),
             (u_hbm, xub.at[pl.ds(TOK, TOK)]),
+            (ids_hbm, ids),
         )
     ):
         copy = pltpu.make_async_copy(src, dst, load_sem.at[k])
         copy.start()
         loads.append(copy)
 
-    ring = [lax.rem(jnp.int32(k) + x, SIDE) for k in FAR]
-    xs = [(k, (y * SIDE + k, t)) for k in ring]
-    ring = [lax.rem(jnp.int32(k) + y, SIDE) for k in FAR]
-    ys = [(k, (k * SIDE + x, t)) for k in ring]
-    ts = []
-    for k in FAR:
-        zk = lax.rem(z + k, SIDE)
-        ts += [(zk * 2, (dp, zk * 2)), (zk * 2 + 1, (dp, zk * 2 + 1))]
-    ts.append((t + 1 - 2 * core, (dp, t + 1 - 2 * core)))
-
-    barrier = pltpu.get_barrier_semaphore()
-    for _, peer in ts + ys + xs:
-        pl.semaphore_signal(barrier, inc=1, device_id=peer, device_id_type=MESH)
-
-    def send(phase, src, dst, peer):
+    def send(phase, src, dst, peer, sem=None):
+        sem = recv_sem.at[phase] if sem is None else sem
         pltpu.make_async_remote_copy(
-            src_ref=src, dst_ref=dst, send_sem=send_sem.at[phase], recv_sem=recv_sem.at[phase], device_id=peer, device_id_type=MESH
+            src_ref=src, dst_ref=dst, send_sem=send_sem.at[phase], recv_sem=sem, device_id=peer, device_id_type=MESH
         ).start()
 
     def arrived(phase, ref, count):
@@ -119,7 +122,8 @@
         whole = ref.at[pl.ds(0, count)]
         pltpu.make_async_copy(whole, whole, send_sem.at[phase]).wait()
 
-    mask = (ids_ref[...] != 0).astype(F32)
+    loads[6].wait()
+    mask = (ids[...] != 0).astype(F32)
     l_send[...] = jnp.broadcast_to(jnp.sum(mask, axis=1, keepdims=True), (1, 128))
     loads[0].wait()
     for k, piece in enumerate(pieces(wt[...])):
@@ -182,25 +186,33 @@
     chunk = total(c_recv, SIDE)
     d_send[...] = chunk
     for _, peer in ys:
-        send(4, d_send, d_recv.at[y], peer)
+        send(4, d_send, d_recv.at[y], peer, slot_sem.at[y])
     d_recv[y] = chunk
-    arrived(4, d_recv, SIDE - 1)
-    acc = jnp.zeros((16, 3 * 128), F32)
-    for k in range(SIDE):
-        part = d_recv[k] - gb[:, k * DCH : (k + 1) * DCH]
-        lf[:, k * DCH : (k + 1) * DCH] = part
+    acc = jnp.zeros((16, 2 * TOK), F32)
+    for k in [y] + [k for k, _ in reversed(ys)]:
+        if k is not y:
+            pltpu.make_async_copy(d_recv.at[k], d_recv.at[k], slot_sem.at[k]).wait()
+        at = pl.ds(pl.multiple_of(k * DCH, DCH), DCH)
+        part = d_recv[k] - gb[:, at]
+        lf[:, at] = part
         part = jnp.concatenate([*pieces(part), jnp.zeros((16 - 3 * OWN, DCH), F32)], axis=0).astype(BF16)
-        acc = acc + nt_dot(part, xub[:, k * DCH : (k + 1) * DCH])
+        lp[:, at] = part
+        acc = acc + nt_dot(part, xub[: 2 * TOK, at])
     acc = acc[:OWN] + acc[OWN : 2 * OWN] + acc[2 * OWN : 3 * OWN]
 
     my_lanes = pl.ds(pl.multiple_of(dp // 2 * 128, 128), 128)
-    tile = jnp.concatenate(
-        [acc[:, :128] * (mask * inv_live), acc[:, 128:256] * INV_TOKENS, lf[:, my_lanes], acc[:, 256:]], axis=0
-    )
+    own = lf[:, my_lanes]
+    tile = jnp.concatenate([acc[:, :TOK] * (mask * inv_live), acc[:, TOK:] * INV_TOKENS, own, own], axis=0)
     g_send[...] = tile
     for _, peer in ts:
         send(5, g_send, g_recv.at[t], peer)
     g_recv[t] = tile
+    own = nt_dot(lp[...], xub[2 * TOK :, :])
+    own = own[:OWN] + own[OWN : 2 * OWN] + own[2 * OWN : 3 * OWN]
+    h_send[...] = own
+    for _, peer in ts:
+        send(12, h_send, h_recv.at[t], peer)
+    h_recv[t] = own
     arrived(5, g_recv, NT - 1)
     for k in range(NT):
         tile = g_recv[k]
@@ -208,7 +220,6 @@
         back[at, :128] = tile[:2]
         back[at, 128:] = tile[2:4]
         mine[at, :] = tile[4:6]
-        crs[at, :] = tile[6:8]
 
     stacked = jnp.concatenate(pieces(back[...]), axis=0).astype(BF16)
 
@@ -222,71 +233,88 @@
         ea_send[k + 1] = part[:, 128:]
     for k, peer in ys:
         send(6, ea_send.at[k], ea_recv.at[y], peer)
+    for h in range(2):
+        part = right_part(ACOLS + h * BCOLS, BCOLS)
+        for k in range(RANK // 8):
+            eb_send[2 * k + h] = part[8 * k : 8 * (k + 1)]
+    for k, peer in xs:
+        send(7, eb_send.at[k], eb_recv.at[x], peer)
+    ea_recv[y] = ea_send[y]
+    eb_recv[x] = eb_send[x]
     half = lax.rem(dp, 2)
     lanes = lax.broadcasted_iota(jnp.int32, (RANK, 128), 1)
     my_rows = jnp.where(lanes // 64 == half, mine[...], 0.0)
     gram = dot32(my_rows, my_rows, ((1,), (1,)))
     gram = jnp.concatenate([gram[8 * k : 8 * (k + 1)] for k in range(RANK // 8)], axis=1)
-    for h in range(2):
-        part = right_part(ACOLS + h * BCOLS, BCOLS)
-        for k in range(RANK // 8):
-            eb_send[2 * k + h, :, :BCOLS] = part[8 * k : 8 * (k + 1)]
-            eb_send[2 * k + h, :, BCOLS:] = gram
-    for k, peer in xs:
-        send(7, eb_send.at[k], eb_recv.at[x], peer)
-    ea_recv[y] = ea_send[y]
-    eb_recv[x] = eb_send[x]
+    p_send[...] = gram
+    for _, peer in xs:
+        send(13, p_send, p_recv.at[x], peer)
+    p_recv[x] = gram
+    arrived(12, h_recv, NT - 1)
+    for k in range(NT):
+        crs[OWN * k : OWN * (k + 1), :] = h_recv[k]
     cross = crs[:, :RANK] + crs[:, RANK : 2 * RANK] + crs[:, 2 * RANK : 3 * RANK]
     cw[...] = dot32(cross, wt[...])
-    arrived(6, ea_recv, SIDE - 1)
-    part = total(ea_recv, SIDE)
-    fa_send[...] = part
-    for _, peer in xs:
-        send(8, fa_send, fa_recv.at[x], peer)
-    fa_recv[x] = part
     arrived(7, eb_recv, SIDE - 1)
     part = total(eb_recv, SIDE)
     fb_send[...] = part
     for _, peer in ys:
         send(9, fb_send, fb_recv.at[y], peer)
     fb_recv[y] = part
+    arrived(6, ea_recv, SIDE - 1)
+    part = total(ea_recv, SIDE)
+    fa_send[...] = part
+    for _, peer in xs:
+        send(8, fa_send, fa_recv.at[x], peer)
+    fa_recv[x] = part
+    arrived(13, p_recv, SIDE - 1)
+    gram = total(p_recv, SIDE)
+    q_send[...] = gram
+    for _, peer in ys:
+        send(14, q_send, q_recv.at[y], peer)
+    q_recv[y] = gram
+    arrived(9, fb_recv, SIDE - 1)
+    part = total(fb_recv, SIDE)
+    gb_send[...] = part
+    for _, peer in xs:
+        send(11, gb_send, gb_recv.at[x], peer)
+    gb_recv[x] = part
     arrived(8, fa_recv, SIDE - 1)
     part = total(fa_recv, SIDE)
     ga_send[...] = part
     for _, peer in ys:
         send(10, ga_send, ga_recv.at[y], peer)
     ga_recv[y] = part
-    arrived(9, fb_recv, SIDE - 1)
-    part = total(fb_recv, SIDE)
-    gb_send[...] = part[:, :BCOLS]
-    for _, peer in xs:
-        send(11, gb_send, gb_recv.at[x], peer)
-    gb_recv[x] = part[:, :BCOLS]
-    packed = part[:, BCOLS:]
+    arrived(14, q_recv, SIDE - 1)
+    packed = total(q_recv, SIDE)
     gram = jnp.concatenate([packed[:, RANK * k : RANK * (k + 1)] for k in range(RANK // 8)], axis=0)
     inverse = inverse_factor(gram)
     basis = dot32(inverse, mine[...])
     rows = dot32(basis, inverse, ((0,), (0,)))
     rows = jnp.where(half == 0, rows[:64], rows[64:])
-    both = jnp.concatenate([inverse, rows], axis=0)
+    high, mid, low = pieces(jnp.concatenate([inverse, rows], axis=0))
+    both = jnp.concatenate([high, high, mid, high, mid, low], axis=1).astype(BF16)
 
     def finish(first, raw):
         width = raw.shape[1]
-        out = dot32(both, raw - cw[:, first : first + width])
+        high, mid, low = pieces(raw - cw[:, first : first + width])
+        right = jnp.concatenate([high, mid, high, low, mid, high], axis=0).astype(BF16)
+        out = jnp.dot(both, right, preferred_element_type=F32)
         nxt_ref[:, first : first + width] = out[:RANK]
         upd_ref[:, first : first + width] = out[RANK:].astype(BF16)
 
+    arrived(11, gb_recv, SIDE - 1)
+    for h in range(2):
+        finish(ACOLS + h * BCOLS, jnp.concatenate([gb_recv[2 * k + h] for k in range(RANK // 8)], axis=0))
     arrived(10, ga_recv, SIDE - 1)
     for k in range(0, SIDE, 2):
         finish(k * 128, jnp.concatenate([ga_recv[k], ga_recv[k + 1]], axis=1))
-    arrived(11, gb_recv, SIDE - 1)
-    for h in range(2):
-        finish(ACOLS + h * BCOLS, jnp.concatenate([gb_recv[2 * k + h] for k in range(RANK // 8)], axis=0))
 
     for phase, (ref, count) in enumerate(
         (
             (a_recv, NT - 1), (l_recv, SIDE - 1), (b_recv, SIDE - 1), (c_recv, SIDE - 1), (d_recv, SIDE - 1), (g_recv, NT - 1),
             (ea_recv, SIDE - 1), (eb_recv, SIDE - 1), (fa_recv, SIDE - 1), (fb_recv, SIDE - 1), (ga_recv, SIDE - 1), (gb_recv, SIDE - 1),
+            (h_recv, NT - 1), (p_recv, SIDE - 1), (q_recv, SIDE - 1),
         )
     ):
         left(phase, ref, count)
@@ -296,12 +324,13 @@
     def vmem(*shape, dtype=F32):
         return pltpu.VMEM(shape, dtype)
 
-    hbm = pl.BlockSpec(memory_space=pl.ANY)
+    operands = (activations, out_grads, token_ids.reshape(1, TOK), prev_acts, prev_grads, prev_basis.T, warm_start.T)
+    hbm = pl.BlockSpec(memory_space=pltpu.HBM)
     local = pl.BlockSpec(memory_space=pltpu.VMEM)
     update, start = pl.pallas_call(
         kernel,
         out_shape=(jax.ShapeDtypeStruct((DIM // REPLICAS, FF), BF16), jax.ShapeDtypeStruct((RANK, FF), F32)),
-        in_specs=[hbm, hbm, local, hbm, hbm, hbm, hbm],
+        in_specs=[hbm] * 7,
         out_specs=(local, local),
         scratch_shapes=[
             vmem(3 * TOK, DIM, dtype=BF16), vmem(3 * TOK, FF, dtype=BF16), vmem(RANK, DIM), vmem(RANK, FF),
@@ -310,16 +339,16 @@
             vmem(OWN, DCH), vmem(SIDE, OWN, DCH), vmem(OWN, DCH), vmem(SIDE, OWN, DCH),
             vmem(OWN, DIM), vmem(OWN, DIM), vmem(8, 128), vmem(NT, 8, 128),
             vmem(RANK, 2 * TOK), vmem(RANK, 128), vmem(RANK, 128), vmem(RANK, FF),
-            vmem(SIDE, RANK, 128), vmem(SIDE, RANK, 128), vmem(SIDE, 8, BCOLS + 128), vmem(SIDE, 8, BCOLS + 128),
-            vmem(RANK, 128), vmem(SIDE, RANK, 128), vmem(8, BCOLS + 128), vmem(SIDE, 8, BCOLS + 128),
+            vmem(SIDE, RANK, 128), vmem(SIDE, RANK, 128), vmem(SIDE, 8, BCOLS), vmem(SIDE, 8, BCOLS),
             vmem(RANK, 128), vmem(SIDE, RANK, 128), vmem(8, BCOLS), vmem(SIDE, 8, BCOLS),
-            pltpu.SemaphoreType.DMA((6,)), pltpu.SemaphoreType.DMA((12,)), pltpu.SemaphoreType.DMA((12,)),
+            vmem(RANK, 128), vmem(SIDE, RANK, 128), vmem(8, BCOLS), vmem(SIDE, 8, BCOLS),
+            vmem(OWN, 128), vmem(NT, OWN, 128), vmem(8, 128), vmem(SIDE, 8, 128), vmem(8, 128), vmem(SIDE, 8, 128), vmem(16, DIM, dtype=BF16),
+            vmem(1, TOK, dtype=jnp.int32), pltpu.SemaphoreType.DMA((7,)), pltpu.SemaphoreType.DMA((15,)),
+            pltpu.SemaphoreType.DMA((15,)), pltpu.SemaphoreType.DMA((SIDE,)),
         ],
         compiler_params=pltpu.CompilerParams(collective_id=0, has_side_effects=True, vmem_limit_bytes=40 * 2**20),
         cost_estimate=pl.CostEstimate(flops=10**9, bytes_accessed=5 * 10**6, transcendentals=0),
-    )(
-        activations, out_grads, token_ids.reshape(1, TOK), prev_acts, prev_grads, prev_basis.T, warm_start.T
-    )
+    )(*(pltpu.with_memory_space_constraint(a, pltpu.HBM) for a in operands))
     return update, start.T
 
 

time: 74.4 us -> 64.6 us (0.87); the launches traced: 73 us -> 64.5 us
  local copies, waits for them, and re-layouts: 8.49 us -> 1.38 us
  Pallas kernels: 63.8 us -> 62.5 us
    unnamed x16 -> x2, local copies, waits for them, and re-layouts: 8.49 us -> 1.38 us
    pallas_call x1, Pallas kernels: 63.8 us -> 62.5 us  [shards(): pl.pallas_call(kernel, out_shape=(jax.ShapeDtypeStruct((DIM // REPLICAS,...]
where the time goes in v2:
time: 64.6 us; the launch traced here: 64.5 us
  Pallas kernels  62.5 us (97%)
  local copies, waits for them, and re-layouts  1.38 us (2%)
    pallas_call x1, Pallas kernels, shards(): pl.pallas_call(kernel, out_shape=(jax.ShapeDtypeStruct((DIM // REPLICAS,...  62.5 us
    unnamed x2, local copies, waits for them, and re-layouts  1.38 us

profile of v2, /device:TPU:1, one launch (start us, length us, event | category | flops | bytes accessed | tf_op | source)
XLA Modules:
  0.0 64.5 jit_solution(9984664087471189448)
XLA Ops:
  0.6 62.5 %shard_map.86 = (bf16[64,1792]{1,0:T(8,128)(2,1)S(1)}, f32[32,1792]{1,0:T(8,128)S(1)}) custom-call(bf16[128,4096]{1,0:T(8,128)(2,1)} %x_hbm.1, bf16[128,1792]{1,0:T(8,128)(2,1)} %y_hbm.1, s32[1,128]{1,0:T(1,128)} %bitcast.7, bf16[128,4096]{1,0:T(8,128)(2,1)} %u_hbm.1, bf16[128,1792]{1,0:T(8,128)(2,1)} %v_hbm.1, f32[32,4096]{1,0:T(8,128)} %bitcast.5, ...), custom_call_target="tpu_custom_call" | custom-call | flops 1000000000 | bytes 5000000 | tf_op jit(solution)/shard_map/pallas_call | solution.py:330
  63.1 0.7 %copy.11 = bf16[64,1792]{1,0:T(8,128)(2,1)} copy(bf16[64,1792]{1,0:T(8,128)(2,1)S(1)} %get-tuple-element.8) | data formatting | bytes 458752
  63.8 0.7 %copy.12 = f32[1792,32]{0,1:T(8,128)} copy(f32[1792,32]{0,1:T(8,128)S(1)} %bitcast.4) | data formatting | bytes 458752

commit v3 on v2

--- a/solution.py
+++ b/solution.py
@@ -318,6 +318,14 @@
         )
     ):
         left(phase, ref, count)
+
+
+def write_out(upd_ref, nxt_ref, upd_out, nxt_out, sem):
+    copies = [pltpu.make_async_copy(upd_ref, upd_out, sem.at[0]), pltpu.make_async_copy(nxt_ref, nxt_out, sem.at[1])]
+    for copy in copies:
+        copy.start()
+    for copy in copies:
+        copy.wait()
 
 
 def shards(activations, out_grads, token_ids, prev_acts, prev_grads, prev_basis, warm_start):
@@ -349,6 +357,13 @@
         compiler_params=pltpu.CompilerParams(collective_id=0, has_side_effects=True, vmem_limit_bytes=40 * 2**20),
         cost_estimate=pl.CostEstimate(flops=10**9, bytes_accessed=5 * 10**6, transcendentals=0),
     )(*(pltpu.with_memory_space_constraint(a, pltpu.HBM) for a in operands))
+    update, start = pl.pallas_call(
+        write_out,
+        out_shape=(jax.ShapeDtypeStruct(update.shape, BF16), jax.ShapeDtypeStruct(start.shape, F32)),
+        in_specs=[local, local],
+        out_specs=(hbm, hbm),
+        scratch_shapes=[pltpu.SemaphoreType.DMA((2,))],
+    )(*(pltpu.with_memory_space_constraint(a, pltpu.VMEM) for a in (update, start)))
     return update, start.T
 
 

time: 64.6 us -> 64 us (level)
  local copies, waits for them, and re-layouts: 1.38 us -> 0 us
  Pallas kernels: 62.5 us -> 63.2 us
    unnamed x2 -> x0, local copies, waits for them, and re-layouts: 1.38 us -> none
    pallas_call x0 -> x1, Pallas kernels: none -> 0.78 us  [shards(): pl.pallas_call(write_out, out_shape=(jax.ShapeDtypeStruct(update.shape, B...]
where the time goes in v3:
time: 64 us; the launch traced here: 63.9 us
  Pallas kernels  63.2 us (99%)
  between operations  0.64 us (1%)
    pallas_call x1, Pallas kernels, shards(): pl.pallas_call(kernel, out_shape=(jax.ShapeDtypeStruct((DIM // REPLICAS,...  62.5 us

profile of v3, /device:TPU:1, one launch (start us, length us, event | category | flops | bytes accessed | tf_op | source)
XLA Modules:
  0.0 63.9 jit_solution(4904995435182053871)
XLA Ops:
  0.6 62.5 %shard_map.86 = (bf16[64,1792]{1,0:T(8,128)(2,1)S(1)}, f32[32,1792]{1,0:T(8,128)S(1)}) custom-call(bf16[128,4096]{1,0:T(8,128)(2,1)} %x_hbm.1, bf16[128,1792]{1,0:T(8,128)(2,1)} %y_hbm.1, s32[1,128]{1,0:T(1,128)} %bitcast.6, bf16[128,4096]{1,0:T(8,128)(2,1)} %u_hbm.1, bf16[128,1792]{1,0:T(8,128)(2,1)} %v_hbm.1, f32[32,4096]{1,0:T(8,128)} %bitcast.4, ...), custom_call_target="tpu_custom_call" | custom-call | flops 1000000000 | bytes 5000000 | tf_op jit(solution)/shard_map/pallas_call | solution.py:338
  63.1 0.8 %shard_map.87 = (bf16[64,1792]{1,0:T(8,128)(2,1)}, f32[32,1792]{1,0:T(8,128)}) custom-call(bf16[64,1792]{1,0:T(8,128)(2,1)S(1)} %get-tuple-element.6.upd_ref, f32[32,1792]{1,0:T(8,128)S(1)} %get-tuple-element.7.nxt_ref), custom_call_target="tpu_custom_call" | custom-call | tf_op jit(solution)/shard_map/pallas_call | solution.py:360
